TPU v7x, 256 devices: a whole 4x4x8 slice. The times are simulated.
256 devices in a mesh: expert: 4 (over y_lo, core), tensor: 64 (over x, y_hi, z).
Axes of the slice: x: 4, y: 4 (y_hi: 2, y_lo: 2; y = y_hi * 2 + y_lo), z: 8, core: 2. Of those that a mesh axis runs over, the one named last changes fastest.
Arguments:
- tokens: bfloat16 [1024, 6144], P('expert', 'tensor'), may hold values from -6 to 6
- expert_ids: int32 [1024, 2], P('expert'), may hold values from 0 to 3, all different within a row; in each aligned block of 256 rows (0 to 255, 256 to 511, ...) at most 192 rows name the same one
- route_gates: float32 [1024, 2], P('expert'), may hold values from 0.2 to 1
- w_gate: bfloat16 [4, 6144, 16384], P('expert', None, 'tensor'), may hold values from -0.078125 to 0.078125
- w_up: bfloat16 [4, 6144, 16384], P('expert', None, 'tensor'), may hold values from -0.078125 to 0.078125
- w_down: bfloat16 [4, 16384, 6144], P('expert', 'tensor'), may hold values from -0.125 to 0.125
Outputs:
- mixed: bfloat16 [1024, 6144], P('expert', 'tensor')
Inputs may be any that keep to these rules, and one draw needn't show every extreme that they name: `expert_ids`: each token names two different experts; in each aligned block of 256 tokens no expert is named by more than 192 tokens, a bound that some block reaches.
All inputs are finite; a program needn't handle non-finite values.
Results may differ from a plain program's by a relative error of at most 0.012.
Values may be sent and summed in bfloat16 or wider, within the bound.
No kernel may reach another device: no remote copies, remote signals or barrier semaphores. Data moves between devices by JAX's collectives and lax.ppermute only.
A program may use at most 128 MiB of HBM per device.

v0:
```python
import jax
import jax.numpy as jnp
from jax import lax
from jax.sharding import PartitionSpec as P

CAP = 192


def body(tokens, expert_ids, route_gates, w_gate, w_up, w_down):
    tok_rows = tokens.shape[0]
    groups = lax.axis_size("expert")
    capacity = CAP
    slot_count = groups * capacity
    gate_local = w_gate[0]
    up_local = w_up[0]
    down_local = w_down[0]
    onehot = (expert_ids[:, :, None] == jnp.arange(groups, dtype=jnp.int32)[None, None, :]).astype(
        jnp.int32
    )
    flattened = onehot.reshape(tok_rows * 2, groups)
    earlier = jnp.cumsum(flattened, axis=0) - flattened
    offsets = jnp.arange(groups, dtype=jnp.int32)[None, :] * capacity
    slot_of = jnp.sum(flattened * (earlier + offsets), axis=1).reshape(tok_rows, 2)
    matches = slot_of[:, :, None] == jnp.arange(slot_count, dtype=jnp.int32)[None, None, :]
    placing = jnp.sum(matches.astype(jnp.float32), axis=1).astype(jnp.bfloat16).T
    combine_weights = jnp.sum(matches.astype(jnp.float32) * route_gates[:, :, None], axis=1)
    outgoing = jnp.dot(placing, tokens, preferred_element_type=jnp.float32).astype(jnp.bfloat16)
    arrived = lax.all_to_all(outgoing, "expert", split_axis=0, concat_axis=0, tiled=True)
    piece = lax.all_gather(arrived, "tensor", axis=1, tiled=True)
    gate = jnp.dot(piece, gate_local, preferred_element_type=jnp.float32)
    up_part = jnp.dot(piece, up_local, preferred_element_type=jnp.float32)
    hidden = (jax.nn.silu(gate) * up_part).astype(jnp.bfloat16)
    summed = lax.psum_scatter(
        lax.dot_general(
            down_local, hidden, (((0,), (1,)), ((), ())), preferred_element_type=jnp.float32
        ),
        "tensor",
        scatter_dimension=0,
        tiled=True,
    )
    outcome = summed.astype(jnp.bfloat16)
    back = lax.all_to_all(outcome, "expert", split_axis=1, concat_axis=1, tiled=True)
    mixed = lax.dot_general(combine_weights, back.astype(jnp.float32), (((1,), (1,)), ((), ())))
    return mixed.astype(jnp.bfloat16)


def solution(mesh):
    in_specs = (
        P("expert", "tensor"),
        P("expert", None),
        P("expert", None),
        P("expert", None, "tensor"),
        P("expert", None, "tensor"),
        P("expert", "tensor", None),
    )
    out_specs = P("expert", "tensor")
    return jax.shard_map(body, mesh=mesh, in_specs=in_specs, out_specs=out_specs, check_vma=False)
```

profile of v0, /device:TPU:1, one launch (start us, length us, event | category | flops | bytes accessed | tf_op | source)
XLA Modules:
  0.0 1115.6 jit_solution(5423483404875156522)
XLA Ops:
  6.5 0.0 copy-start
  6.5 0.0 all-gather.2.cloned.1.call-start
  6.5 1.0 copy.20
  7.5 0.1 eq.45
  7.7 0.1 eq.41
  7.8 1.2 reduce-window.6
  9.0 0.2 slice_reduce_fusion
  9.3 0.2 reduce-window.9
  9.4 0.1 add_bitcast_fusion
  9.5 0.1 fusion.23
  9.6 0.1 eq.49
  9.8 0.1 copy.22
  9.8 1.1 convert_reduce_fusion
  10.9 1.7 convolution_convert_fusion
  12.6 1.8 all_to_all.16
  14.4 0.9 copy.23
  15.3 10.2 all_to_all.24
  25.5 0.8 copy.24
  26.3 1.8 all_to_all.18
  28.1 0.0 all-gather.2.cloned.1.call-update
  28.1 0.0 reduce-scatter.4.cloned.1.call-start
  28.2 153.2 %all-gather.2.cloned.1.call-done = bf16[768,6144]{0,1:T(8,128)(2,1)} async-done(((bf16[768,96]{0,1:T(8,128)(2,1)}), bf16[768,6144]{0,1:T(8,128)(2,1)}) %all-gather.2.cloned.1.call-update) | async-done | bytes 9437200 | tf_op jit(solution)/shard_map/all_gather | solution.py:29
  181.4 8.1 fusion.3
  189.5 0.0 copy-done
  189.5 21.1 %convolution_bitcast_fusion = f32[6144,768]{0,1:T(8,128)} fusion(bf16[1,256,6144]{2,1,0:T(8,128)(2,1)S(1)} %copy-done, bf16[768,6144]{0,1:T(8,128)(2,1)} %all-gather.2.cloned.1.call-done, bf16[1,6144,256]{2,1,0:T(8,128)(2,1)} %param.10, f32[768,256]{1,0:T(8,128)} %fusion.3), kind=kOutput, calls=%fused_computation | convolution fusion | flops 4833017856 | bytes 35389440 | tf_op jit(solution)/shard_map/dot_general | solution.py:34
  210.6 18.7 %copy.25 = f32[6144,768]{1,0:T(8,128)} copy(f32[6144,768]{0,1:T(8,128)} %convolution_bitcast_fusion) | data formatting | bytes 37748736
  229.4 0.0 reduce-scatter.4.cloned.1.call-update
  229.4 863.8 %reduce-scatter.4.cloned.1.call-done = f32[96,768]{1,0:T(8,128)} async-done(((f32[6144,768]{1,0:T(8,128)}), f32[96,768]{1,0:T(8,128)}) %reduce-scatter.4.cloned.1.call-update) | async-done | bytes 294928
  1093.1 1.8 copy.26
  1094.9 13.0 %all_to_all.25 = bf16[96,4,192]{0,2,1:T(8,128)(2,1)S(1)} all-to-all(bf16[96,4,192]{0,2,1:T(8,128)(2,1)} %bitcast.54), channel_id=1, replica_groups=mesh['expert'=4,'tensor'=64] {'expert'}, dimensions={1} | all-to-all | bytes 294912 | tf_op jit(solution)/shard_map/all_to_all | solution.py:42
  1107.9 0.9 fusion.26
  (2 shorter events, 0.0 us)
Async XLA Ops:
  6.5 183.0 %copy-start = (bf16[1,256,6144]{2,1,0:T(8,128)(2,1)S(1)}, bf16[1,256,6144]{2,1,0:T(8,128)(2,1)}, u32[]{:S(2)}) copy-start(bf16[1,256,6144]{2,1,0:T(8,128)(2,1)} %param.11) | copy-start | bytes 9437188
  6.5 174.9 %all-gather.2.cloned.1.call-start = ((), (), s32[]{:S(2)}) async-start(), calls=%async_computation.3 | async-start | bytes 9584640 | tf_op jit(solution)/shard_map/all_gather | solution.py:29
  28.1 1065.0 %reduce-scatter.4.cloned.1.call-start = ((), (), s32[]{:S(2)}) async-start(), calls=%async_computation.4 | async-start | bytes 19169280
Sparse Core Ops, SparseCore 0:
  28.3 153.1 all-gather.1
  229.5 863.5 reduce-scatter.3
where the time goes:
time: 1120 us
  waiting for transfers between devices  1020 us (91%)
  matrix products  31.8 us (3%)
  local copies, waits for them, and re-layouts  27.5 us (2%)
  blocking collectives  23.2 us (2%)
  between operations  13.4 us (1%)
    unnamed x3, waiting for transfers between devices  864 us
    all_gather x1, waiting for transfers between devices, body(): piece = lax.all_gather(arrived, 'tensor', axis=1, tiled=True)  153 us
  transfers between devices with their start and end apart: 2, of which 2 were waited for; matrix products, arithmetic and copies ran while one was open for 0% of the time, Pallas kernels for 0%

commit v1 on v0

--- a/solution.py
+++ b/solution.py
@@ -26,7 +26,9 @@
     combine_weights = jnp.sum(matches.astype(jnp.float32) * route_gates[:, :, None], axis=1)
     outgoing = jnp.dot(placing, tokens, preferred_element_type=jnp.float32).astype(jnp.bfloat16)
     arrived = lax.all_to_all(outgoing, "expert", split_axis=0, concat_axis=0, tiled=True)
-    piece = lax.all_gather(arrived, "tensor", axis=1, tiled=True)
+    piece = jnp.concatenate(
+        lax.all_to_all(jnp.stack([arrived] * lax.axis_size("tensor")), "tensor", 0, 0), axis=1
+    )
     gate = jnp.dot(piece, gate_local, preferred_element_type=jnp.float32)
     up_part = jnp.dot(piece, up_local, preferred_element_type=jnp.float32)
     hidden = (jax.nn.silu(gate) * up_part).astype(jnp.bfloat16)

time: 1120 us -> 1180 us (1.054)
  blocking collectives: 23.2 us -> 242 us
  waiting for transfers between devices: 1020 us -> 865 us
    all_to_all x0 -> x1, blocking collectives: none -> 220 us  [body(): lax.all_to_all(jnp.stack([arrived] * lax.axis_size('tensor')), 'tensor',...]
    all_gather x1 -> x0, waiting for transfers between devices: 153 us -> none  [body(): piece = lax.all_gather(arrived, 'tensor', axis=1, tiled=True)]
    unnamed x5 -> x11, local copies, waits for them, and re-layouts: 21.4 us -> 25.2 us
    unnamed x3 -> x2, waiting for transfers between devices: 864 us -> 865 us
  transfers between devices with their start and end apart: 2 -> 1, of which waited for: 2 -> 1; matrix products, arithmetic and copies ran while one was open for 0% -> 0% of each run, Pallas kernels for 0% -> 0%
where the time goes in v1:
time: 1180 us
  waiting for transfers between devices  865 us (73%)
  blocking collectives  242 us (21%)
  local copies, waits for them, and re-layouts  33.3 us (3%)
  matrix products  27.2 us (2%)
  between operations  13.5 us (1%)
    unnamed x2, waiting for transfers between devices  865 us
    all_to_all x1, blocking collectives, body(): lax.all_to_all(jnp.stack([arrived] * lax.axis_size('tensor')), 'tensor',...  220 us
    unnamed x11, local copies, waits for them, and re-layouts  25.2 us
  transfers between devices with their start and end apart: 1, of which 1 were waited for; matrix products, arithmetic and copies ran while one was open for 0% of the time, Pallas kernels for 0%

profile of v1, /device:TPU:1, one launch (start us, length us, event | category | flops | bytes accessed | tf_op | source)
XLA Modules:
  0.0 1183.5 jit_solution(11602427868070632741)
XLA Ops:
  6.5 0.0 copy-start
  6.5 1.0 copy.21
  7.5 0.1 eq.45
  7.7 0.1 eq.41
  7.8 1.2 reduce-window.6
  9.0 0.2 slice_reduce_fusion
  9.3 0.2 reduce-window.9
  9.4 0.1 add_bitcast_fusion
  9.5 0.1 fusion.23
  9.6 0.1 eq.49
  9.8 0.1 copy.23
  9.8 1.1 convert_reduce_fusion
  10.9 1.7 convolution_convert_fusion
  12.6 1.8 all_to_all.17
  14.4 0.9 copy.24
  15.3 10.2 all_to_all.26
  25.5 0.8 copy.25
  26.3 1.8 stack.4
  28.1 2.0 stack.5
  30.2 0.0 copy-start.3
  30.2 219.5 %all_to_all.27 = bf16[64,768,96]{1,2,0:T(8,128)(2,1)S(1)} all-to-all(bf16[64,768,96]{1,2,0:T(8,128)(2,1)S(1)} %stack.5), channel_id=1, replica_groups=mesh['expert'=4,'tensor'=64] {'tensor'}, dimensions={0} | all-to-all | bytes 18874368 | tf_op jit(solution)/shard_map/all_to_all | solution.py:30
  249.7 3.7 copy-done.2
  253.4 3.5 fusion.3
  256.9 21.1 %convolution_bitcast_fusion = f32[6144,768]{0,1:T(8,128)} fusion(bf16[1,256,6144]{2,1,0:T(8,128)(2,1)S(1)} %copy-done, bf16[768,6144]{0,1:T(8,128)(2,1)} %bitcast.57, bf16[1,6144,256]{2,1,0:T(8,128)(2,1)} %param.10, f32[768,256]{1,0:T(8,128)} %fusion.3), kind=kOutput, calls=%fused_computation | convolution fusion | flops 4833017856 | bytes 35389440 | tf_op jit(solution)/shard_map/dot_general | solution.py:36
  278.0 18.7 %copy.26 = f32[6144,768]{1,0:T(8,128)} copy(f32[6144,768]{0,1:T(8,128)} %convolution_bitcast_fusion) | data formatting | bytes 37748736
  296.8 0.0 reduce-scatter.4.cloned.1.call-update
  296.8 0.0 copy-start.1
  296.8 864.7 %reduce-scatter.4.cloned.1.call-done = f32[96,768]{1,0:T(8,128)} async-done(((f32[6144,768]{1,0:T(8,128)}), f32[96,768]{1,0:T(8,128)}) %reduce-scatter.4.cloned.1.call-update) | async-done | bytes 294928
  1161.5 1.8 copy.27
  1163.3 12.4 %all_to_all.28 = bf16[96,4,192]{0,2,1:T(8,128)(2,1)S(1)} all-to-all(bf16[96,4,192]{0,2,1:T(8,128)(2,1)} %bitcast.59), channel_id=1, replica_groups=mesh['expert'=4,'tensor'=64] {'expert'}, dimensions={1} | all-to-all | bytes 294912 | tf_op jit(solution)/shard_map/all_to_all | solution.py:44
  1175.7 0.9 fusion.26
  1176.6 0.0 copy-done.1
  (6 shorter events, 0.0 us)
Async XLA Ops:
  6.5 250.4 %copy-start = (bf16[1,256,6144]{2,1,0:T(8,128)(2,1)S(1)}, bf16[1,256,6144]{2,1,0:T(8,128)(2,1)}, u32[]{:S(2)}) copy-start(bf16[1,256,6144]{2,1,0:T(8,128)(2,1)} %param.11) | copy-start | bytes 9437188
  6.5 1155.0 %reduce-scatter.4.cloned.1.call-start = ((), (), s32[]{:S(2)}) async-start(), calls=%async_computation.4 | async-start | bytes 19169280
  30.2 223.3 %copy-start.3 = (bf16[1,6144,256]{2,1,0:T(8,128)(2,1)S(1)}, bf16[1,6144,256]{2,1,0:T(8,128)(2,1)}, u32[]{:S(2)}) copy-start(bf16[1,6144,256]{2,1,0:T(8,128)(2,1)} %param.9) | copy-start | bytes 9437188
  249.7 3.7 copy-start.2
  296.8 879.9 %copy-start.1 = (bf16[1,256,6144]{2,1,0:T(8,128)(2,1)S(1)}, bf16[1,256,6144]{2,1,0:T(8,128)(2,1)}, u32[]{:S(2)}) copy-start(bf16[1,256,6144]{2,1,0:T(8,128)(2,1)} %param.11) | copy-start | bytes 9437188
Sparse Core Ops, SparseCore 0:
  296.9 864.5 reduce-scatter.3
